TPU v7x, 32 devices: a whole 2x2x4 slice. The times are simulated.
32 devices in a mesh: groups: 2 (over y), blk: 4 (over z), feat: 4 (over x, core).
Axes of the slice: x: 2, y: 2, z: 4, core: 2. Of those that a mesh axis runs over, the one named last changes fastest.
Arguments:
- queries: bfloat16 [512, 16384], P(('groups', 'blk'), 'feat'), parts along dimension 0, may hold values from -6 to 6
- train_grads: bfloat16 [4096, 16384], P(('groups', 'blk'), 'feat'), parts along dimension 0, may hold values from -6 to 6
- precond: float32 [16384], P('feat'), may hold values from 0.3 to 27
- counts: int32 [8], P(('groups', 'blk')), parts along dimension 0, may hold values from 128 to 512, as said below
- segment_ids: int32 [512], P('groups'), parts along dimension 0, may hold values from 0 to 127, as said below
- flagged: int32 [128], P('groups'), parts along dimension 0, may hold values from 0 to 127, as said below
Outputs:
- attribution: float32 [4096, 64], P(('groups', 'blk', 'feat')), parts along dimension 0
There are 2 independent parts, one for each index of `groups`. A program takes and returns all parts, laid end to end along the dimension named above; an argument that names none is the same for every part. Nothing has to cross between parts.
Inputs may be any that keep to these rules, and one draw needn't show every extreme that they name: counts[k] is the number of live rows of shard k; one shard is full. `segment_ids`: segment ids never fall; every segment of 0 to 127 holds at least one row; each block of 64 consecutive query rows holds exactly 32 rows of flagged segments. `flagged`: distinct segments; together they hold exactly 128 query rows.
All inputs are finite; a program needn't handle non-finite values.
Results may differ from a plain program's by a relative error of at most 0.0028.
Values may be sent and summed in bfloat16 or wider, within the bound.
A program may use at most 64 MiB of HBM per device.

v0:
```python
import math

import jax
import jax.numpy as jnp
from jax import lax
from jax.sharding import PartitionSpec as P

F = 16384


epsilon = 1e-06


def label_max(scores, row_segments, flagged):
    label_count = flagged.shape[0]
    block = math.gcd(label_count, 8)

    def block_max(labels_block):
        member = row_segments[None, :] == labels_block[:, None]
        masked = jnp.where(member[:, :, None], scores[None, :, :], -jnp.inf)
        return jnp.max(masked, axis=1)

    result = lax.map(block_max, flagged.reshape(label_count // block, block))
    return result.reshape(label_count, scores.shape[1])


def per_device(queries, train_grads, precond, counts, segment_ids, flagged):
    query_full = queries.astype(jnp.float32)
    query_sq = jnp.sum(query_full * query_full * precond[None, :], axis=1)
    train_full = train_grads.astype(jnp.float32)
    train_sq = jnp.sum(train_full * train_full * precond[None, :], axis=1)
    query_total, train_total = lax.psum((query_sq, train_sq), "feat")
    normed = (query_full * precond[None, :] * lax.rsqrt(query_total + epsilon)[:, None]).astype(
        jnp.bfloat16
    )
    shard_rows = train_grads.shape[0]
    partial_scores = lax.dot_general(
        lax.all_gather(normed, "blk", axis=0, tiled=True),
        train_grads,
        (((1,), (1,)), ((), ())),
        preferred_element_type=jnp.float32,
    )
    reduced = lax.psum_scatter(partial_scores, "feat", scatter_dimension=1, tiled=True)
    width = shard_rows // lax.axis_size("feat")
    feat_index = lax.axis_index("feat")
    own_sq = lax.dynamic_slice_in_dim(train_total, feat_index * width, width)
    scaled = reduced * (math.sqrt(F) * lax.rsqrt(own_sq + epsilon))[None, :]
    pooled = label_max(scaled, segment_ids, flagged)
    local_rows = feat_index * width + jnp.arange(width, dtype=jnp.int32)
    live = local_rows < counts[0]
    return jnp.where(live[:, None], pooled.T, jnp.float32(0.0))


def solution(mesh):
    return jax.shard_map(
        per_device,
        mesh=mesh,
        in_specs=(
            P(("groups", "blk"), "feat"),
            P(("groups", "blk"), "feat"),
            P("feat"),
            P(("groups", "blk")),
            P("groups"),
            P("groups"),
        ),
        out_specs=P(("groups", "blk", "feat"), None),
        check_vma=False,
    )
```

profile of v0, /device:TPU:0, one launch (start us, length us, event | category | flops | bytes accessed | tf_op | source)
XLA Modules:
  0.0 103.6 jit_solution(3010986801825816817)
XLA Ops:
  6.5 3.4 %multiply_reduce_fusion = f32[512]{0:T(512)S(1)} fusion(bf16[512,4096]{1,0:T(8,128)(2,1)} %param.9, f32[4096]{0:T(1024)} %param.10), kind=kLoop, calls=%fused_computation.5 | loop fusion | flops 8388096 | bytes 4212736 | tf_op jit(solution)/shard_map/reduce_sum | solution.py:31
  10.0 0.2 fusion.4
  10.2 8.3 %all-reduce = (f32[64]{0:T(128)S(1)}, f32[512]{0:T(512)S(1)}) all-reduce(f32[64]{0:T(128)S(1)} %fusion.4, f32[512]{0:T(512)S(1)} %multiply_reduce_fusion), channel_id=1, replica_groups=mesh['groups'=2,'blk'=4,'feat'=4] {'feat'}, use_global_device_ids=true, to_apply=%region_1.0 | all-reduce | flops 576 | bytes 4608 | tf_op jit(solution)/shard_map/psum | solution.py:32
  18.6 1.0 fusion.2
  19.5 0.0 all-gather.2.cloned.1.call-update
  19.5 0.0 copy-start.3
  19.6 0.0 reduce-scatter.2.cloned.1.call-start
  19.6 46.3 %all-gather.2.cloned.1.call-done = bf16[256,4096]{1,0:T(8,128)(2,1)} async-done(((bf16[64,4096]{1,0:T(8,128)(2,1)}), bf16[256,4096]{1,0:T(8,128)(2,1)}) %all-gather.2.cloned.1.call-update) | async-done | bytes 2097168 | tf_op jit(solution)/shard_map/all_gather | solution.py:38
  66.0 4.9 %fusion.6 = f32[256,512]{1,0:T(8,128)} fusion(bf16[256,4096]{1,0:T(8,128)(2,1)} %all-gather.2.cloned.1.call-done, bf16[512,4096]{1,0:T(8,128)(2,1)} %param.9), kind=kOutput, calls=%fused_computation.18 | convolution fusion | flops 1073741824 | bytes 6815744 | tf_op jit(solution)/shard_map/dot_general | solution.py:37
  70.9 0.0 reduce-scatter.2.cloned.1.call-update
  70.9 0.1 reshape.46
  71.7 0.1 rsqrt_multiply_fusion
  71.7 19.7 %reduce-scatter.2.cloned.1.call-done = f32[256,128]{1,0:T(8,128)} async-done(((f32[256,512]{1,0:T(8,128)}), f32[256,128]{1,0:T(8,128)}) %reduce-scatter.2.cloned.1.call-update) | async-done | bytes 131088 | tf_op jit(solution)/shard_map/reduce_scatter | solution.py:43
  91.4 0.9 broadcast_multiply_fusion
  92.3 3.8 %while.10 = (s32[]{:T(128)}, f32[8,8,128]{2,1,0:T(8,128)S(1)}, s32[256]{0:T(256)S(1)}, s32[8,8]{1,0:T(8,128)S(1)}, f32[256,128]{1,0:T(8,128)S(1)}, /*index=5*/s32[]{:T(128)}) while((s32[]{:T(128)}, f32[8,8,128]{2,1,0:T(8,128)S(1)}, s32[256]{0:T(256)S(1)}, s32[8,8]{1,0:T(8,128)S(1)}, f32[256,128]{1,0:T(8,128)S(1)}, /*index=5*/s32[]{:T(128)}) %tuple.25), condition=%wide.region_7.8_spmd, body=%wide.region_5.7_spmd.sunk | while | flops 525314 | bytes 148653 | solution.py:23
  92.3 0.1 broadcast_compare_fusion.2
  92.4 0.3 select_reduce_fusion.2
  92.8 0.1 broadcast_compare_fusion.2
  92.9 0.3 select_reduce_fusion.2
  93.3 0.1 broadcast_compare_fusion.2
  93.4 0.3 select_reduce_fusion.2
  93.8 0.1 broadcast_compare_fusion.2
  93.8 0.3 select_reduce_fusion.2
  94.2 0.1 broadcast_compare_fusion.2
  94.3 0.3 select_reduce_fusion.2
  94.7 0.1 broadcast_compare_fusion.2
  94.8 0.3 select_reduce_fusion.2
  95.2 0.1 broadcast_compare_fusion.2
  95.3 0.3 select_reduce_fusion.2
  95.7 0.1 broadcast_compare_fusion.2
  95.7 0.3 select_reduce_fusion.2
  96.1 0.6 fusion.5
  (27 shorter events, 0.2 us)
Async XLA Ops:
  6.5 3.4 %copy-start.1 = (f32[4096]{0:T(1024)S(1)}, f32[4096]{0:T(1024)}, u32[]{:S(2)}) copy-start(f32[4096]{0:T(1024)} %param.10) | copy-start | bytes 49156
  6.5 3.4 %copy-start = (bf16[64,4096]{1,0:T(8,128)(2,1)S(1)}, bf16[64,4096]{1,0:T(8,128)(2,1)}, u32[]{:S(2)}) copy-start(bf16[64,4096]{1,0:T(8,128)(2,1)} %param.8) | copy-start | bytes 1572868
  6.5 59.4 %all-gather.2.cloned.1.call-start = ((), (), s32[]{:S(2)}) async-start(), calls=%async_computation.1 | async-start | bytes 2621440 | tf_op jit(solution)/shard_map/all_gather | solution.py:38
  19.5 51.4 %copy-start.3 = (s32[64]{0:T(128)S(1)}, s32[64]{0:T(128)}, u32[]{:S(2)}) copy-start(s32[64]{0:T(128)} %param.13) | copy-start | bytes 772
  19.6 72.8 %copy-start.2 = (s32[256]{0:T(256)S(1)}, s32[256]{0:T(256)}, u32[]{:S(2)}) copy-start(s32[256]{0:T(256)} %param.12) | copy-start | bytes 3076
  19.6 71.8 %reduce-scatter.2.cloned.1.call-start = ((), (), s32[]{:S(2)}) async-start(), calls=%async_computation.2 | async-start | bytes 655360 | tf_op jit(solution)/shard_map/reduce_scatter | solution.py:43
Sparse Core Ops, SparseCore 0:
  19.7 46.2 all-gather.1
  71.0 20.3 reduce-scatter.1
where the time goes:
time: 104 us
  waiting for transfers between devices  66 us (63%)
  between operations  14.1 us (14%)
  other arithmetic  9.62 us (9%)
  blocking collectives  8.34 us (8%)
  matrix products  4.9 us (5%)
    all_gather x1, waiting for transfers between devices, per_device(): lax.all_gather(normed, 'blk', axis=0, tiled=True)  46.3 us
    reduce_scatter x1, waiting for transfers between devices, per_device(): lax.psum_scatter(partial_scores, 'feat', scatter_dimension=1, tiled=True)  19.7 us
    psum x1, blocking collectives, per_device(): query_total, train_total = lax.psum((query_sq, train_sq), 'feat')  8.34 us
    dot_general x1, matrix products, per_device(): lax.dot_general(lax.all_gather(normed, 'blk', axis=0, tiled=True), train_...  4.9 us
    reduce_sum x1, other arithmetic, per_device(): train_sq = jnp.sum(train_full * train_full * precond[None, :], axis=1)  3.41 us
    reduce_max x8, other arithmetic, block_max(): return jnp.max(masked, axis=1)  2.78 us
  transfers between devices with their start and end apart: 2, of which 2 were waited for; matrix products, arithmetic and copies ran while one was open for 0% of the time, Pallas kernels for 0%

commit v1 on v0

v1 whole, which is shorter than its diff:
```python
import functools
import math

import jax
import jax.numpy as jnp
from jax import lax
from jax.experimental import pallas as pl
from jax.experimental.pallas import tpu as pltpu
from jax.sharding import PartitionSpec as P

F = 16384
epsilon = 1e-06
MESH = pl.DeviceIdType.MESH
f32 = jnp.float32


def iota(shape, dim):
    return lax.broadcasted_iota(jnp.int32, shape, dim)


def kernel(
    n, nf, C,
    q_hbm, t_hbm, p_ref, counts_ref, seg_ref, flagged_ref, flag_smem,
    out_ref,
    q_vmem, t_vmem, gath, onehot, segcol, acc, qacc, tacc, tsq, send, recv, pooled,
    q_sem, t_sem, zsend, zrecv, fsend, frecv,
):
    me = lax.axis_index("blk")
    myf = lax.axis_index("feat")
    rows = q_vmem.shape[0]
    half = rows // 2
    K = q_vmem.shape[1]
    kc = K // C
    T = t_vmem.shape[1]
    w = T // nf
    labels = flagged_ref.shape[1]

    barrier = pltpu.get_barrier_semaphore()

    @pl.when(me > 0)
    def _():
        pl.semaphore_signal(barrier, inc=1, device_id={"blk": me - 1}, device_id_type=MESH)

    @pl.when(me < n - 1)
    def _():
        pl.semaphore_signal(barrier, inc=1, device_id={"blk": me + 1}, device_id_type=MESH)

    for j in range(1, nf):
        pl.semaphore_signal(
            barrier, inc=1, device_id={"feat": lax.rem(myf + j, nf)}, device_id_type=MESH
        )

    q_copy = pltpu.make_async_copy(q_hbm, q_vmem, q_sem)
    q_copy.start()
    t_copies = []
    for c in range(C):
        t_copies.append(
            pltpu.make_async_copy(t_hbm.at[:, c * kc : (c + 1) * kc], t_vmem.at[c], t_sem.at[c])
        )
        t_copies[-1].start()

    flag_row = flagged_ref[...].astype(f32)
    eye = iota((labels, labels), 0) == iota((labels, labels), 1)
    flag_col = jnp.sum(jnp.where(eye, flag_row, 0.0), axis=1, keepdims=True)
    before = (iota((rows, rows), 0) < iota((rows, rows), 1)).astype(f32)
    for b in range(n):
        seg_row = seg_ref[:, b * rows : (b + 1) * rows].astype(f32)
        member = jnp.max(jnp.where(flag_col == seg_row, 1.0, 0.0), axis=0, keepdims=True)
        place = jnp.dot(
            jnp.broadcast_to(member, (8, rows)), before, preferred_element_type=f32
        )[0:1]
        slot = iota((half, rows), 0).astype(f32)
        hot = jnp.where((slot == place) & (member > 0.5), 1.0, 0.0)
        onehot[b] = hot
        ids = jnp.sum(hot * seg_row, axis=1, keepdims=True)
        segcol[b] = jnp.broadcast_to(ids, (half, w)).astype(jnp.int32)

    q_copy.wait()
    hot_me = onehot[me].astype(jnp.bfloat16)

    def zcopy(b, c, d):
        return pltpu.make_async_remote_copy(
            src_ref=gath.at[b, c],
            dst_ref=gath.at[b, c],
            send_sem=zsend.at[d, b, c],
            recv_sem=zrecv.at[b, c],
            device_id={"blk": me + (2 * d - 1)},
            device_id_type=MESH,
        )

    for c in range(C):
        picked = jnp.dot(
            hot_me, q_vmem[:, c * kc : (c + 1) * kc], preferred_element_type=f32
        )
        gath[me, c] = picked.astype(jnp.bfloat16)
        if c == 0:
            arrivals = (nf - 1) + jnp.where(me > 0, 1, 0) + jnp.where(me < n - 1, 1, 0)
            pl.semaphore_wait(barrier, arrivals)

        @pl.when(me > 0)
        def _():
            zcopy(me, c, 0).start()

        @pl.when(me < n - 1)
        def _():
            zcopy(me, c, 1).start()

    for t_copy in t_copies:
        t_copy.wait()

    def norm_rows(g, carry):
        base = pl.multiple_of(g * 32, 32)
        total = jnp.zeros((32, 128), f32)
        for c in range(C):
            for j in range(kc // 128):
                t = t_vmem[c, pl.ds(base, 32), j * 128 : (j + 1) * 128].astype(f32)
                at = c * kc + j * 128
                total = total + t * t * p_ref[:, at : at + 128]
        tacc[pl.ds(base, 32), :] = total
        return carry

    lax.fori_loop(0, T // 32, norm_rows, 0)
    for i in range(T // 128):
        turned = jnp.transpose(tacc[i * 128 : (i + 1) * 128, :])
        tsq[:, i * 128 : (i + 1) * 128] = jnp.sum(turned, axis=0, keepdims=True)

    def clear(d):
        acc[d] = jnp.zeros(acc.shape[1:], f32)
        qacc[d] = jnp.zeros(qacc.shape[1:], f32)

    def work(b, c, d):
        q = gath[b, c].astype(f32)
        x = q * p_ref[:, pl.ds(pl.multiple_of(c * kc, 128), kc)]
        hi = x.astype(jnp.bfloat16)
        lo = (x - hi.astype(f32)).astype(jnp.bfloat16)
        both = jnp.concatenate([hi, lo], axis=0)
        acc[d] += lax.dot_general(
            both, t_vmem[c], (((1,), (1,)), ((), ())), preferred_element_type=f32
        )
        sq = x * q
        total = qacc[d]
        for j in range(kc // 128):
            total = total + sq[:, j * 128 : (j + 1) * 128]
        qacc[d] = total

    def fcopy(b, f):
        return pltpu.make_async_remote_copy(
            src_ref=send.at[b, f],
            dst_ref=recv.at[b, myf],
            send_sem=fsend.at[b, f],
            recv_sem=frecv.at[b, myf],
            device_id={"feat": f},
            device_id_type=MESH,
        )

    def arrived(b, f):
        return pltpu.make_async_remote_copy(
            src_ref=recv.at[b, f],
            dst_ref=recv.at[b, f],
            send_sem=fsend.at[b, f],
            recv_sem=frecv.at[b, f],
            device_id={"feat": f},
            device_id_type=MESH,
        )

    diagonal = iota((half, w), 0) == iota((half, w), 1)

    def finish(b, d):
        s = acc[d, 0:half, :] + acc[d, half : 2 * half, :]
        q_col = jnp.sum(qacc[d], axis=1, keepdims=True)
        q_row = jnp.sum(jnp.where(diagonal, q_col, 0.0), axis=0, keepdims=True)
        t_row = tsq[...]
        line = iota((8, w), 0)
        for f in range(nf):
            cut = slice(f * w, (f + 1) * w)
            send[b, f, 0:half, :] = s[:, cut]
            send[b, f, half : half + 8, :] = jnp.where(
                line == 0, q_row, jnp.where(line == 1, t_row[:, cut], 0.0)
            )
        for j in range(1, nf):
            fcopy(b, lax.rem(myf + j, nf)).start()

    def collect(b):
        total = send[b, myf]
        for j in range(1, nf):
            f = lax.rem(myf + j, nf)
            arrived(b, f).wait_recv()
            total = total + recv[b, f]
        q_row = total[half : half + 1, :]
        q_col = jnp.sum(jnp.where(diagonal, q_row, 0.0), axis=1, keepdims=True)
        s = total[0:half, :] * lax.rsqrt(q_col + epsilon)
        ids = segcol[b]

        def one_label(l8, carry):
            base = pl.multiple_of(l8 * 8, 8)
            best = [
                jnp.max(jnp.where(ids == flag_smem[base + i], s, -jnp.inf), axis=0, keepdims=True)
                for i in range(8)
            ]
            best = jnp.concatenate(best, axis=0)
            pooled[pl.ds(base, 8), 0:w] = jnp.maximum(pooled[pl.ds(base, 8), 0:w], best)
            return carry

        lax.fori_loop(0, labels // 8, one_label, 0)
        return total[half + 1 : half + 2, :]

    pooled[...] = jnp.full(pooled.shape, -jnp.inf, f32)
    clear(0)

    def own(c, carry):
        work(me, c, 0)
        return carry

    lax.fori_loop(0, C, own, 0)
    finish(me, 0)

    def collect_step(s):
        @pl.when(me - s >= 0)
        def _():
            collect(me - s)

        @pl.when(me + s < n)
        def _():
            collect(me + s)

    def step(s, carry):
        low, high = me - s, me + s
        clear(0)
        clear(1)

        def chunk(c, inner):
            @pl.when(low >= 0)
            def _():
                zcopy(low, c, 1).wait_recv()

                @pl.when(me < n - 1)
                def _():
                    zcopy(low, c, 1).start()

            @pl.when(high < n)
            def _():
                zcopy(high, c, 0).wait_recv()

                @pl.when(me > 0)
                def _():
                    zcopy(high, c, 0).start()

            @pl.when(low >= 0)
            def _():
                work(low, c, 0)

            @pl.when(high < n)
            def _():
                work(high, c, 1)

            return inner

        lax.fori_loop(0, C, chunk, 0)

        @pl.when(low >= 0)
        def _():
            finish(low, 0)

        @pl.when(high < n)
        def _():
            finish(high, 1)

        @pl.when(s > 1)
        def _():
            collect_step(s - 1)

        return carry

    lax.fori_loop(1, n, step, 0)
    collect_step(n - 1)
    t_total = collect(me)

    scale = math.sqrt(F) * lax.rsqrt(t_total + epsilon)
    live = (myf * w + iota((1, w), 1)) < counts_ref[0]
    pooled[0:labels, 0:w] = jnp.where(live, pooled[0:labels, 0:w] * scale, 0.0)
    turned = jnp.transpose(pooled[...])
    out_ref[...] = turned[0:w, 0:labels]

    def drain_block(b, carry):
        for j in range(1, nf):
            fcopy(b, lax.rem(myf + j, nf)).wait_send()

        def drain_chunk(c, inner):
            @pl.when((me > 0) & (b >= me))
            def _():
                zcopy(b, c, 0).wait_send()

            @pl.when((me < n - 1) & (b <= me))
            def _():
                zcopy(b, c, 1).wait_send()

            return inner

        lax.fori_loop(0, C, drain_chunk, 0)
        return carry

    lax.fori_loop(0, n, drain_block, 0)


def per_device(n, nf, queries, train_grads, precond, counts, segment_ids, flagged):
    rows, K = queries.shape
    T = train_grads.shape[0]
    w = T // nf
    half = rows // 2
    labels = flagged.shape[0]
    C = 4
    kc = K // C
    vmem = pl.BlockSpec(memory_space=pltpu.VMEM)
    smem = pl.BlockSpec(memory_space=pltpu.SMEM)
    hbm = pl.BlockSpec(memory_space=pl.ANY)
    return pl.pallas_call(
        functools.partial(kernel, n, nf, C),
        out_shape=jax.ShapeDtypeStruct((w, labels), f32),
        in_specs=[hbm, hbm, vmem, smem, vmem, vmem, smem],
        out_specs=vmem,
        scratch_shapes=[
            pltpu.VMEM((rows, K), jnp.bfloat16),
            pltpu.VMEM((C, T, kc), jnp.bfloat16),
            pltpu.VMEM((n, C, half, kc), jnp.bfloat16),
            pltpu.VMEM((n, half, rows), f32),
            pltpu.VMEM((n, half, w), jnp.int32),
            pltpu.VMEM((2, 2 * half, T), f32),
            pltpu.VMEM((2, half, 128), f32),
            pltpu.VMEM((T, 128), f32),
            pltpu.VMEM((1, T), f32),
            pltpu.VMEM((n, nf, half + 8, w), f32),
            pltpu.VMEM((n, nf, half + 8, w), f32),
            pltpu.VMEM((128, 128), f32),
            pltpu.SemaphoreType.DMA,
            pltpu.SemaphoreType.DMA((C,)),
            pltpu.SemaphoreType.DMA((2, n, C)),
            pltpu.SemaphoreType.DMA((n, C)),
            pltpu.SemaphoreType.DMA((n, nf)),
            pltpu.SemaphoreType.DMA((n, nf)),
        ],
        compiler_params=pltpu.CompilerParams(
            collective_id=0, has_side_effects=True, vmem_limit_bytes=48 * 1024 * 1024
        ),
    )(
        queries,
        train_grads,
        precond.reshape(1, K),
        counts,
        segment_ids.reshape(1, -1),
        flagged.reshape(1, -1),
        flagged,
    )


def solution(mesh):
    return jax.shard_map(
        functools.partial(per_device, mesh.shape["blk"], mesh.shape["feat"]),
        mesh=mesh,
        in_specs=(
            P(("groups", "blk"), "feat"),
            P(("groups", "blk"), "feat"),
            P("feat"),
            P(("groups", "blk")),
            P("groups"),
            P("groups"),
        ),
        out_specs=P(("groups", "blk", "feat"), None),
        check_vma=False,
    )
```

time: 104 us -> 35 us (0.34)
  waiting for transfers between devices: 66 us -> 0 us
  Pallas kernels: 0 us -> 28.1 us
  between operations: 14.1 us -> 0.67 us
  other arithmetic: 9.62 us -> 0 us
  blocking collectives: 8.34 us -> 0 us
  local copies, waits for them, and re-layouts: 0.22 us -> 5.97 us
  matrix products: 4.9 us -> 0 us
    all_gather x1 -> x0, waiting for transfers between devices: 46.3 us -> none  [per_device(): lax.all_gather(normed, 'blk', axis=0, tiled=True)]
    pallas_call x0 -> x1, Pallas kernels: none -> 28.1 us  [per_device(): pl.pallas_call(functools.partial(kernel, n, nf, C), out_shape=jax.ShapeDt...]
    reduce_scatter x1 -> x0, waiting for transfers between devices: 19.7 us -> none  [per_device(): lax.psum_scatter(partial_scores, 'feat', scatter_dimension=1, tiled=True)]
    psum x1 -> x0, blocking collectives: 8.34 us -> none  [per_device(): query_total, train_total = lax.psum((query_sq, train_sq), 'feat')]
    unnamed x8 -> x10, local copies, waits for them, and re-layouts: 0.02 us -> 5.27 us
    dot_general x1 -> x0, matrix products: 4.9 us -> none  [per_device(): lax.dot_general(lax.all_gather(normed, 'blk', axis=0, tiled=True), train_...]
    reduce_sum x2 -> x0, other arithmetic: 3.66 us -> none  [the longest x1 3.41 us: per_device(): train_sq = jnp.sum(train_full * train_full * precond[None, :], axis=1)]
    reduce_max x8 -> x0, other arithmetic: 2.78 us -> none  [block_max(): return jnp.max(masked, axis=1)]
  transfers between devices with their start and end apart: 2 -> 0, of which waited for: 2 -> 0; matrix products, arithmetic and copies ran while one was open for 0% -> 0% of each run, Pallas kernels for 0% -> 0%
where the time goes in v1:
time: 35 us; the launch traced here: 34.7 us
  Pallas kernels  28.1 us (80%)
  local copies, waits for them, and re-layouts  5.97 us (17%)
  between operations  0.67 us (2%)
    pallas_call x1, Pallas kernels, per_device(): pl.pallas_call(functools.partial(kernel, n, nf, C), out_shape=jax.ShapeDt...  28.1 us
    unnamed x10, local copies, waits for them, and re-layouts  5.27 us

profile of v1, /device:TPU:0, one launch (start us, length us, event | category | flops | bytes accessed | tf_op | source)
XLA Modules:
  0.0 34.7 jit_solution(11017150668327823548)
XLA Ops:
  0.7 0.0 copy-start
  0.7 2.2 %copy-done = bf16[512,4096]{1,0:T(8,128)(2,1)S(1)} copy-done((bf16[512,4096]{1,0:T(8,128)(2,1)S(1)}, bf16[512,4096]{1,0:T(8,128)(2,1)}, u32[]{:S(2)}) %copy-start) | copy-done | bytes 4194328
  2.8 0.0 copy-start.1
  2.8 1.0 %copy-done.1 = bf16[64,4096]{1,0:T(8,128)(2,1)S(1)} copy-done((bf16[64,4096]{1,0:T(8,128)(2,1)S(1)}, bf16[64,4096]{1,0:T(8,128)(2,1)}, u32[]{:S(2)}) %copy-start.1) | copy-done | bytes 524312
  3.9 0.0 copy-start.2
  3.9 0.7 %copy-done.2 = f32[4096]{0:T(1024)S(1)} copy-done((f32[4096]{0:T(1024)S(1)}, f32[4096]{0:T(1024)}, u32[]{:S(2)}) %copy-start.2) | copy-done | bytes 16408
  4.6 0.0 copy-start.3
  4.6 0.7 %copy-done.3 = s32[64]{0:T(128)S(1)} copy-done((s32[64]{0:T(128)S(1)}, s32[64]{0:T(128)}, u32[]{:S(2)}) %copy-start.3) | copy-done | bytes 280
  5.3 0.0 copy-start.4
  5.3 0.7 %copy-done.4 = s32[256]{0:T(256)S(1)} copy-done((s32[256]{0:T(256)S(1)}, s32[256]{0:T(256)}, u32[]{:S(2)}) %copy-start.4) | copy-done | bytes 1048
  5.9 28.1 %shard_map.64 = f32[128,64]{1,0:T(8,128)S(1)} custom-call(bf16[64,4096]{1,0:T(8,128)(2,1)S(1)} %copy-done.1, bf16[512,4096]{1,0:T(8,128)(2,1)S(1)} %copy-done, f32[1,4096]{1,0:T(1,128)S(1)} %bitcast.3, s32[1]{0:T(128)S(6)} %copy.8.counts_ref, s32[1,256]{1,0:T(1,128)S(1)} %bitcast.5, s32[1,64]{1,0:T(1,128)S(1)} %bitcast.4, s32[64]{0:T(128)S(1)} %copy-done.3), custom_call_target="tpu_custom_call" | custom-call | tf_op jit(solution)/shard_map/pallas_call | solution.py:316
  34.0 0.7 %copy.7 = f32[128,64]{0,1:T(8,128)} copy(f32[128,64]{1,0:T(8,128)S(1)} %shard_map.64) | data formatting | bytes 65536 | tf_op jit(solution)/shard_map/pallas_call | solution.py:316
Async XLA Ops:
  0.7 2.2 %copy-start = (bf16[512,4096]{1,0:T(8,128)(2,1)S(1)}, bf16[512,4096]{1,0:T(8,128)(2,1)}, u32[]{:S(2)}) copy-start(bf16[512,4096]{1,0:T(8,128)(2,1)} %t_hbm.1) | copy-start | bytes 12582916
  2.8 1.0 %copy-start.1 = (bf16[64,4096]{1,0:T(8,128)(2,1)S(1)}, bf16[64,4096]{1,0:T(8,128)(2,1)}, u32[]{:S(2)}) copy-start(bf16[64,4096]{1,0:T(8,128)(2,1)} %q_hbm.1) | copy-start | bytes 1572868
  3.9 0.7 %copy-start.2 = (f32[4096]{0:T(1024)S(1)}, f32[4096]{0:T(1024)}, u32[]{:S(2)}) copy-start(f32[4096]{0:T(1024)} %param.8) | copy-start | bytes 49156
  4.6 0.7 %copy-start.3 = (s32[64]{0:T(128)S(1)}, s32[64]{0:T(128)}, u32[]{:S(2)}) copy-start(s32[64]{0:T(128)} %flag_smem.1) | copy-start | bytes 772
  5.3 0.7 %copy-start.4 = (s32[256]{0:T(256)S(1)}, s32[256]{0:T(256)}, u32[]{:S(2)}) copy-start(s32[256]{0:T(256)} %param.10) | copy-start | bytes 3076

commit v2 on v1

--- a/solution.py
+++ b/solution.py
@@ -20,9 +20,10 @@
 
 def kernel(
     n, nf, C,
-    q_hbm, t_hbm, p_ref, counts_ref, seg_ref, flagged_ref, flag_smem,
+    q_hbm, t_hbm, p_hbm, counts_hbm, seg_hbm, flagged_hbm,
     out_ref,
-    q_vmem, t_vmem, gath, onehot, segcol, acc, qacc, tacc, tsq, send, recv, pooled,
+    p_ref, counts_ref, seg_ref, flagged_ref, flag_smem, small_sem,
+    q_vmem, t_vmem, gath, onehot, segcol, acc, qacc, tacc, tsq, t_total, send, recv, pooled,
     q_sem, t_sem, zsend, zrecv, fsend, frecv,
 ):
     me = lax.axis_index("blk")
@@ -50,6 +51,20 @@
             barrier, inc=1, device_id={"feat": lax.rem(myf + j, nf)}, device_id_type=MESH
         )
 
+    small_copies = [
+        pltpu.make_async_copy(src, dst, small_sem.at[i])
+        for i, (src, dst) in enumerate(
+            (
+                (seg_hbm, seg_ref),
+                (flagged_hbm, flagged_ref),
+                (p_hbm, p_ref),
+                (flagged_hbm, flag_smem),
+                (counts_hbm, counts_ref),
+            )
+        )
+    ]
+    for small in small_copies[:2]:
+        small.start()
     q_copy = pltpu.make_async_copy(q_hbm, q_vmem, q_sem)
     q_copy.start()
     t_copies = []
@@ -58,6 +73,11 @@
             pltpu.make_async_copy(t_hbm.at[:, c * kc : (c + 1) * kc], t_vmem.at[c], t_sem.at[c])
         )
         t_copies[-1].start()
+
+    for small in small_copies[2:]:
+        small.start()
+    for small in small_copies[:2]:
+        small.wait()
 
     flag_row = flagged_ref[...].astype(f32)
     eye = iota((labels, labels), 0) == iota((labels, labels), 1)
@@ -105,8 +125,8 @@
         def _():
             zcopy(me, c, 1).start()
 
-    for t_copy in t_copies:
-        t_copy.wait()
+    for waiting in small_copies[2:] + t_copies:
+        waiting.wait()
 
     def norm_rows(g, carry):
         base = pl.multiple_of(g * 32, 32)
@@ -194,15 +214,15 @@
         def one_label(l8, carry):
             base = pl.multiple_of(l8 * 8, 8)
             best = [
-                jnp.max(jnp.where(ids == flag_smem[base + i], s, -jnp.inf), axis=0, keepdims=True)
+                jnp.max(jnp.where(ids == flag_smem[0, base + i], s, -jnp.inf), axis=0, keepdims=True)
                 for i in range(8)
             ]
             best = jnp.concatenate(best, axis=0)
-            pooled[pl.ds(base, 8), 0:w] = jnp.maximum(pooled[pl.ds(base, 8), 0:w], best)
+            pooled[pl.ds(base, 8), :] = jnp.maximum(pooled[pl.ds(base, 8), :], best)
             return carry
 
         lax.fori_loop(0, labels // 8, one_label, 0)
-        return total[half + 1 : half + 2, :]
+        t_total[...] = total[half + 1 : half + 2, :]
 
     pooled[...] = jnp.full(pooled.shape, -jnp.inf, f32)
     clear(0)
@@ -265,6 +285,10 @@
         def _():
             finish(high, 1)
 
+        @pl.when(s == 1)
+        def _():
+            collect(me)
+
         @pl.when(s > 1)
         def _():
             collect_step(s - 1)
@@ -273,13 +297,10 @@
 
     lax.fori_loop(1, n, step, 0)
     collect_step(n - 1)
-    t_total = collect(me)
-
-    scale = math.sqrt(F) * lax.rsqrt(t_total + epsilon)
+
+    scale = math.sqrt(F) * lax.rsqrt(t_total[...] + epsilon)
     live = (myf * w + iota((1, w), 1)) < counts_ref[0]
-    pooled[0:labels, 0:w] = jnp.where(live, pooled[0:labels, 0:w] * scale, 0.0)
-    turned = jnp.transpose(pooled[...])
-    out_ref[...] = turned[0:w, 0:labels]
+    out_ref[...] = jnp.where(live, pooled[...] * scale, 0.0)
 
     def drain_block(b, carry):
         for j in range(1, nf):
@@ -311,14 +332,19 @@
     C = 4
     kc = K // C
     vmem = pl.BlockSpec(memory_space=pltpu.VMEM)
-    smem = pl.BlockSpec(memory_space=pltpu.SMEM)
-    hbm = pl.BlockSpec(memory_space=pl.ANY)
-    return pl.pallas_call(
+    hbm = pl.BlockSpec(memory_space=pltpu.HBM)
+    pooled = pl.pallas_call(
         functools.partial(kernel, n, nf, C),
-        out_shape=jax.ShapeDtypeStruct((w, labels), f32),
-        in_specs=[hbm, hbm, vmem, smem, vmem, vmem, smem],
+        out_shape=jax.ShapeDtypeStruct((labels, w), f32),
+        in_specs=[hbm] * 6,
         out_specs=vmem,
         scratch_shapes=[
+            pltpu.VMEM((1, K), f32),
+            pltpu.SMEM((1,), jnp.int32),
+            pltpu.VMEM((1, n * rows), jnp.int32),
+            pltpu.VMEM((1, labels), jnp.int32),
+            pltpu.SMEM((1, labels), jnp.int32),
+            pltpu.SemaphoreType.DMA((5,)),
             pltpu.VMEM((rows, K), jnp.bfloat16),
             pltpu.VMEM((C, T, kc), jnp.bfloat16),
             pltpu.VMEM((n, C, half, kc), jnp.bfloat16),
@@ -328,9 +354,10 @@
             pltpu.VMEM((2, half, 128), f32),
             pltpu.VMEM((T, 128), f32),
             pltpu.VMEM((1, T), f32),
+            pltpu.VMEM((1, w), f32),
             pltpu.VMEM((n, nf, half + 8, w), f32),
             pltpu.VMEM((n, nf, half + 8, w), f32),
-            pltpu.VMEM((128, 128), f32),
+            pltpu.VMEM((labels, w), f32),
             pltpu.SemaphoreType.DMA,
             pltpu.SemaphoreType.DMA((C,)),
             pltpu.SemaphoreType.DMA((2, n, C)),
@@ -339,7 +366,7 @@
             pltpu.SemaphoreType.DMA((n, nf)),
         ],
         compiler_params=pltpu.CompilerParams(
-            collective_id=0, has_side_effects=True, vmem_limit_bytes=48 * 1024 * 1024
+            collective_id=0, has_side_effects=True, vmem_limit_bytes=63 * 1024 * 1024
         ),
     )(
         queries,
@@ -348,8 +375,8 @@
         counts,
         segment_ids.reshape(1, -1),
         flagged.reshape(1, -1),
-        flagged,
     )
+    return pooled.T
 
 
 def solution(mesh):

time: 35 us -> 30.8 us (0.88)
  local copies, waits for them, and re-layouts: 5.97 us -> 1.38 us
  Pallas kernels: 28.1 us -> 28.6 us
    unnamed x10 -> x1, local copies, waits for them, and re-layouts: 5.27 us -> 1.38 us
    pallas_call x1 -> x0, local copies, waits for them, and re-layouts: 0.7 us -> none  [per_device(): pl.pallas_call(functools.partial(kernel, n, nf, C), out_shape=jax.ShapeDt...]
    pallas_call x1, Pallas kernels: 28.1 us -> 28.6 us  [per_device(): pl.pallas_call(functools.partial(kernel, n, nf, C), out_shape=jax.ShapeDt...]
where the time goes in v2:
time: 30.8 us; the launch traced here: 30.7 us
  Pallas kernels  28.6 us (93%)
  local copies, waits for them, and re-layouts  1.38 us (4%)
  between operations  0.66 us (2%)
    pallas_call x1, Pallas kernels, per_device(): pl.pallas_call(functools.partial(kernel, n, nf, C), out_shape=jax.ShapeDt...  28.6 us
    unnamed x1, local copies, waits for them, and re-layouts  1.38 us

profile of v2, /device:TPU:0, one launch (start us, length us, event | category | flops | bytes accessed | tf_op | source)
XLA Modules:
  0.0 30.7 jit_solution(7094401119638727452)
XLA Ops:
  0.7 28.6 %shard_map.64 = f32[64,128]{1,0:T(8,128)} custom-call(bf16[64,4096]{1,0:T(8,128)(2,1)} %q_hbm.1, bf16[512,4096]{1,0:T(8,128)(2,1)} %t_hbm.1, f32[1,4096]{1,0:T(1,128)} %bitcast.5, s32[1]{0:T(128)S(6)} %copy.8.counts_hbm, s32[1,256]{1,0:T(1,128)} %bitcast.6, s32[1,64]{1,0:T(1,128)} %bitcast.7), custom_call_target="tpu_custom_call" | custom-call | tf_op jit(solution)/shard_map/pallas_call | solution.py:336
  29.3 1.4 %copy.9 = f32[128,64]{0,1:T(8,128)} copy(f32[128,64]{0,1:T(8,128)} %bitcast.4) | data formatting | bytes 65536

commit v3 on v2

v3 whole, which is shorter than its diff:
```python
import functools
import math

import jax
import jax.numpy as jnp
from jax import lax
from jax.experimental import pallas as pl
from jax.experimental.pallas import tpu as pltpu
from jax.sharding import PartitionSpec as P

F = 16384
epsilon = 1e-06
MESH = pl.DeviceIdType.MESH
f32 = jnp.float32


def iota(shape, dim):
    return lax.broadcasted_iota(jnp.int32, shape, dim)


def kernel(
    n, nf, C, pieces,
    q_hbm, t_hbm, p_hbm, counts_hbm, seg_hbm, flagged_hbm,
    out_ref,
    p_ref, counts_ref, seg_ref, flagged_ref, small_sem,
    q_vmem, t_vmem, gath, segcol, acc, qacc, tacc, tsq, t_total, send, recv, pooled, flagcol, scored,
    q_sem, t_sem, zsend, zrecv, fsend, frecv,
):
    me = lax.axis_index("blk")
    myf = lax.axis_index("feat")
    rows = q_vmem.shape[0]
    half = rows // 2
    K = q_vmem.shape[1]
    kc = K // C
    T = t_vmem.shape[1]
    w = T // nf
    labels = flagged_ref.shape[1]

    small_copies = [
        pltpu.make_async_copy(src, dst, small_sem.at[i])
        for i, (src, dst) in enumerate(
            (
                (seg_hbm, seg_ref),
                (flagged_hbm, flagged_ref),
                (p_hbm, p_ref),
                (counts_hbm, counts_ref),
            )
        )
    ]
    for small in small_copies[:2]:
        small.start()
    barrier = pltpu.get_barrier_semaphore()

    @pl.when(me > 0)
    def _():
        pl.semaphore_signal(barrier, inc=1, device_id={"blk": me - 1}, device_id_type=MESH)

    @pl.when(me < n - 1)
    def _():
        pl.semaphore_signal(barrier, inc=1, device_id={"blk": me + 1}, device_id_type=MESH)

    for j in range(1, nf):
        pl.semaphore_signal(
            barrier, inc=1, device_id={"feat": lax.rem(myf + j, nf)}, device_id_type=MESH
        )

    q_copy = pltpu.make_async_copy(q_hbm, q_vmem, q_sem)
    q_copy.start()
    t_copies = []
    for c in range(C):
        t_copies.append(
            pltpu.make_async_copy(t_hbm.at[:, c * kc : (c + 1) * kc], t_vmem.at[c], t_sem.at[c])
        )
        t_copies[-1].start()

    for small in small_copies[2:]:
        small.start()
    for small in small_copies[:2]:
        small.wait()

    flag_row = flagged_ref[...].astype(f32)
    eye = iota((labels, labels), 0) == iota((labels, labels), 1)
    flag_col = jnp.sum(jnp.where(eye, flag_row, 0.0), axis=1, keepdims=True)
    before = (iota((rows, rows), 0) < iota((rows, rows), 1)).astype(f32)
    slot = iota((half, rows), 0).astype(f32)

    def select(seg_row):
        member = jnp.max(jnp.where(flag_col == seg_row, 1.0, 0.0), axis=0, keepdims=True)
        place = jnp.dot(
            jnp.broadcast_to(member, (8, rows)), before, preferred_element_type=f32
        )[0:1]
        return jnp.where((slot == place) & (member > 0.5), 1.0, 0.0)

    seg_rows = [seg_ref[:, b * rows : (b + 1) * rows].astype(f32) for b in range(n)]
    seg_me = seg_rows[0]
    for b in range(1, n):
        seg_me = jnp.where(me == b, seg_rows[b], seg_me)
    hot_me = select(seg_me).astype(jnp.bfloat16)
    q_copy.wait()

    def zcopy(b, piece, d):
        cs = pl.ds(pieces[piece][0], pieces[piece][1])
        return pltpu.make_async_remote_copy(
            src_ref=gath.at[b, cs],
            dst_ref=gath.at[b, cs],
            send_sem=zsend.at[d, b, piece],
            recv_sem=zrecv.at[b, piece],
            device_id={"blk": me + (2 * d - 1)},
            device_id_type=MESH,
        )

    for i, (start, count) in enumerate(pieces):
        for c in range(start, start + count):
            picked = jnp.dot(
                hot_me, q_vmem[:, c * kc : (c + 1) * kc], preferred_element_type=f32
            )
            gath[me, c] = picked.astype(jnp.bfloat16)
        if i == 0:
            arrivals = (nf - 1) + jnp.where(me > 0, 1, 0) + jnp.where(me < n - 1, 1, 0)
            pl.semaphore_wait(barrier, arrivals)

        @pl.when(me > 0)
        def _():
            zcopy(me, i, 0).start()

        @pl.when(me < n - 1)
        def _():
            zcopy(me, i, 1).start()

    flagcol[...] = jnp.broadcast_to(flag_col, (labels, w))
    for b in range(n):
        ids = jnp.sum(select(seg_rows[b]) * seg_rows[b], axis=1, keepdims=True)
        segcol[b] = jnp.broadcast_to(ids, (half, w))

    for waiting in small_copies[2:] + t_copies:
        waiting.wait()

    def norm_rows(g, carry):
        base = pl.multiple_of(g * 32, 32)
        total = jnp.zeros((32, 128), f32)
        for c in range(C):
            for j in range(kc // 128):
                t = t_vmem[c, pl.ds(base, 32), j * 128 : (j + 1) * 128].astype(f32)
                at = c * kc + j * 128
                total = total + t * t * p_ref[:, at : at + 128]
        tacc[pl.ds(base, 32), :] = total
        return carry

    def norm_total():
        for i in range(T // 128):
            turned = jnp.transpose(tacc[i * 128 : (i + 1) * 128, :])
            tsq[:, i * 128 : (i + 1) * 128] = jnp.sum(turned, axis=0, keepdims=True)

    def clear(d):
        acc[d] = jnp.zeros(acc.shape[1:], f32)
        qacc[d] = jnp.zeros(qacc.shape[1:], f32)

    def work(b, c, d):
        q = gath[b, c].astype(f32)
        x = q * p_ref[:, pl.ds(pl.multiple_of(c * kc, 128), kc)]
        hi = x.astype(jnp.bfloat16)
        lo = (x - hi.astype(f32)).astype(jnp.bfloat16)
        both = jnp.concatenate([hi, lo], axis=0)
        acc[d] += lax.dot_general(
            both, t_vmem[c], (((1,), (1,)), ((), ())), preferred_element_type=f32
        )
        sq = x * q
        total = qacc[d]
        for j in range(kc // 128):
            total = total + sq[:, j * 128 : (j + 1) * 128]
        qacc[d] = total

    def fcopy(b, f):
        return pltpu.make_async_remote_copy(
            src_ref=send.at[b, f],
            dst_ref=recv.at[b, myf],
            send_sem=fsend.at[b, f],
            recv_sem=frecv.at[b, myf],
            device_id={"feat": f},
            device_id_type=MESH,
        )

    def arrived(b, f):
        return pltpu.make_async_remote_copy(
            src_ref=recv.at[b, f],
            dst_ref=recv.at[b, f],
            send_sem=fsend.at[b, f],
            recv_sem=frecv.at[b, f],
            device_id={"feat": f},
            device_id_type=MESH,
        )

    diagonal = iota((half, w), 0) == iota((half, w), 1)

    def finish(b, d):
        s = acc[d, 0:half, :] + acc[d, half : 2 * half, :]
        q_col = jnp.sum(qacc[d], axis=1, keepdims=True)
        q_row = jnp.sum(jnp.where(diagonal, q_col, 0.0), axis=0, keepdims=True)
        t_row = tsq[...]
        line = iota((8, w), 0)
        for f in range(nf):
            cut = slice(f * w, (f + 1) * w)
            send[b, f, 0:half, :] = s[:, cut]
            send[b, f, half : half + 8, :] = jnp.where(
                line == 0, q_row, jnp.where(line == 1, t_row[:, cut], 0.0)
            )
        for j in (*range(2, nf), 1):
            fcopy(b, lax.rem(myf + j, nf)).start()

    def collect(b):
        total = send[b, myf]
        for j in range(1, nf):
            f = lax.rem(myf + j, nf)
            arrived(b, f).wait_recv()
            total = total + recv[b, f]
        q_row = total[half : half + 1, :]
        q_col = jnp.sum(jnp.where(diagonal, q_row, 0.0), axis=1, keepdims=True)
        scored[...] = total[0:half, :] * lax.rsqrt(q_col + epsilon)
        names = flagcol[...]

        def some_rows(g, best):
            for i in range(8):
                r = pl.ds(g * 8 + i, 1)
                best = jnp.maximum(
                    best, jnp.where(names == segcol[b, r, :], scored[r, :], -jnp.inf)
                )
            return best

        pooled[...] = lax.fori_loop(0, half // 8, some_rows, pooled[...])
        t_total[...] = total[half + 1 : half + 2, :]

    pooled[...] = jnp.full(pooled.shape, -jnp.inf, f32)

    def collect_step(s):
        def side(d, carry):
            b = me + (2 * d - 1) * s

            @pl.when((b >= 0) & (b < n))
            def _():
                collect(b)

            return carry

        lax.fori_loop(0, 2, side, 0)

    def step(s, carry):
        low, high = me - s, me + s
        clear(0)
        clear(1)

        @pl.when(s == 1)
        def _():
            clear(2)

        for i, (start, count) in enumerate(pieces):
            @pl.when(low >= 0)
            def _():
                zcopy(low, i, 1).wait_recv()

                @pl.when(me < n - 1)
                def _():
                    zcopy(low, i, 1).start()

            @pl.when(high < n)
            def _():
                zcopy(high, i, 0).wait_recv()

                @pl.when(me > 0)
                def _():
                    zcopy(high, i, 0).start()

            def chunk(c, inner):
                @pl.when(s == 1)
                def _():
                    quarter = T // 32 // C
                    lax.fori_loop(c * quarter, (c + 1) * quarter, norm_rows, 0)
                    work(me, c, 2)

                @pl.when(low >= 0)
                def _():
                    work(low, c, 0)

                @pl.when(high < n)
                def _():
                    work(high, c, 1)

                return inner

            lax.fori_loop(start, start + count, chunk, 0)

            if i == max(len(pieces) - 2, 0):
                @pl.when(s == 2)
                def _():
                    collect(me)

                @pl.when(s > 1)
                def _():
                    collect_step(s - 1)

        @pl.when(s == 1)
        def _():
            norm_total()
            finish(me, 2)

        @pl.when(low >= 0)
        def _():
            finish(low, 0)

        @pl.when(high < n)
        def _():
            finish(high, 1)

        return carry

    lax.fori_loop(1, n, step, 0)
    if n == 2:
        collect(me)

    def drain_block(b, carry):
        for j in range(1, nf):
            fcopy(b, lax.rem(myf + j, nf)).wait_send()

        for i in range(len(pieces)):
            @pl.when((me > 0) & (b >= me))
            def _():
                zcopy(b, i, 0).wait_send()

            @pl.when((me < n - 1) & (b <= me))
            def _():
                zcopy(b, i, 1).wait_send()

        return carry

    lax.fori_loop(0, n, drain_block, 0)

    collect_step(n - 1)

    scale = math.sqrt(F) * lax.rsqrt(t_total[...] + epsilon)
    live = (myf * w + iota((1, w), 1)) < counts_ref[0]
    out_ref[...] = jnp.where(live, pooled[...] * scale, 0.0)


def per_device(n, nf, queries, train_grads, precond, counts, segment_ids, flagged):
    rows, K = queries.shape
    T = train_grads.shape[0]
    w = T // nf
    half = rows // 2
    labels = flagged.shape[0]
    C = 4
    pieces = ((0, 1), (1, 1), (2, 1), (3, 1))
    kc = K // C
    vmem = pl.BlockSpec(memory_space=pltpu.VMEM)
    hbm = pl.BlockSpec(memory_space=pltpu.HBM)
    pooled = pl.pallas_call(
        functools.partial(kernel, n, nf, C, pieces),
        out_shape=jax.ShapeDtypeStruct((labels, w), f32),
        in_specs=[hbm] * 6,
        out_specs=vmem,
        scratch_shapes=[
            pltpu.VMEM((1, K), f32),
            pltpu.SMEM((1,), jnp.int32),
            pltpu.VMEM((1, n * rows), jnp.int32),
            pltpu.VMEM((1, labels), jnp.int32),
            pltpu.SemaphoreType.DMA((4,)),
            pltpu.VMEM((rows, K), jnp.bfloat16),
            pltpu.VMEM((C, T, kc), jnp.bfloat16),
            pltpu.VMEM((n, C, half, kc), jnp.bfloat16),
            pltpu.VMEM((n, half, w), f32),
            pltpu.VMEM((3, 2 * half, T), f32),
            pltpu.VMEM((3, half, 128), f32),
            pltpu.VMEM((T, 128), f32),
            pltpu.VMEM((1, T), f32),
            pltpu.VMEM((1, w), f32),
            pltpu.VMEM((n, nf, half + 8, w), f32),
            pltpu.VMEM((n, nf, half + 8, w), f32),
            pltpu.VMEM((labels, w), f32),
            pltpu.VMEM((labels, w), f32),
            pltpu.VMEM((half, w), f32),
            pltpu.SemaphoreType.DMA,
            pltpu.SemaphoreType.DMA((C,)),
            pltpu.SemaphoreType.DMA((2, n, len(pieces))),
            pltpu.SemaphoreType.DMA((n, len(pieces))),
            pltpu.SemaphoreType.DMA((n, nf)),
            pltpu.SemaphoreType.DMA((n, nf)),
        ],
        compiler_params=pltpu.CompilerParams(
            collective_id=0, has_side_effects=True, vmem_limit_bytes=63 * 1024 * 1024
        ),
    )(
        queries,
        train_grads,
        precond.reshape(1, K),
        counts,
        segment_ids.reshape(1, -1),
        flagged.reshape(1, -1),
    )
    return pooled.T


def solution(mesh):
    return jax.shard_map(
        functools.partial(per_device, mesh.shape["blk"], mesh.shape["feat"]),
        mesh=mesh,
        in_specs=(
            P(("groups", "blk"), "feat"),
            P(("groups", "blk"), "feat"),
            P("feat"),
            P(("groups", "blk")),
            P("groups"),
            P("groups"),
        ),
        out_specs=P(("groups", "blk", "feat"), None),
        check_vma=False,
    )
```

time: 30.8 us -> 30.4 us (0.987)
  Pallas kernels: 28.6 us -> 28.2 us
    pallas_call x1, Pallas kernels: 28.6 us -> 28.2 us  [per_device(): pl.pallas_call(functools.partial(kernel, n, nf, C, pieces), out_shape=jax...]
where the time goes in v3:
time: 30.4 us; the launch traced here: 30.2 us
  Pallas kernels  28.2 us (93%)
  local copies, waits for them, and re-layouts  1.38 us (5%)
  between operations  0.66 us (2%)
    pallas_call x1, Pallas kernels, per_device(): pl.pallas_call(functools.partial(kernel, n, nf, C, pieces), out_shape=jax...  28.2 us
    unnamed x1, local copies, waits for them, and re-layouts  1.38 us

profile of v3, /device:TPU:0, one launch (start us, length us, event | category | flops | bytes accessed | tf_op | source)
XLA Modules:
  0.0 30.2 jit_solution(5236465292803327994)
XLA Ops:
  0.7 28.2 %shard_map.64 = f32[64,128]{1,0:T(8,128)} custom-call(bf16[64,4096]{1,0:T(8,128)(2,1)} %q_hbm.1, bf16[512,4096]{1,0:T(8,128)(2,1)} %t_hbm.1, f32[1,4096]{1,0:T(1,128)} %bitcast.5, s32[1]{0:T(128)S(6)} %copy.8.counts_hbm, s32[1,256]{1,0:T(1,128)} %bitcast.6, s32[1,64]{1,0:T(1,128)} %bitcast.7), custom_call_target="tpu_custom_call" | custom-call | tf_op jit(solution)/shard_map/pallas_call | solution.py:354
  28.9 1.4 %copy.9 = f32[128,64]{0,1:T(8,128)} copy(f32[128,64]{0,1:T(8,128)} %bitcast.4) | data formatting | bytes 65536

commit v4 on v3

--- a/solution.py
+++ b/solution.py
@@ -253,6 +253,14 @@
             clear(2)
 
         for i, (start, count) in enumerate(pieces):
+            @pl.when(high < n)
+            def _():
+                zcopy(high, i, 0).wait_recv()
+
+                @pl.when(me > 0)
+                def _():
+                    zcopy(high, i, 0).start()
+
             @pl.when(low >= 0)
             def _():
                 zcopy(low, i, 1).wait_recv()
@@ -260,14 +268,6 @@
                 @pl.when(me < n - 1)
                 def _():
                     zcopy(low, i, 1).start()
-
-            @pl.when(high < n)
-            def _():
-                zcopy(high, i, 0).wait_recv()
-
-                @pl.when(me > 0)
-                def _():
-                    zcopy(high, i, 0).start()
 
             def chunk(c, inner):
                 @pl.when(s == 1)

time: 30.4 us -> 30.4 us (level)
  no operation moved by 1% of the time
where the time goes in v4:
time: 30.4 us; the launch traced here: 30.2 us
  Pallas kernels  28.2 us (93%)
  local copies, waits for them, and re-layouts  1.38 us (5%)
  between operations  0.66 us (2%)
    pallas_call x1, Pallas kernels, per_device(): pl.pallas_call(functools.partial(kernel, n, nf, C, pieces), out_shape=jax...  28.2 us
    unnamed x1, local copies, waits for them, and re-layouts  1.38 us

profile of v4, /device:TPU:0, one launch (start us, length us, event | category | flops | bytes accessed | tf_op | source)
XLA Modules:
  0.0 30.2 jit_solution(11956608346124791255)
XLA Ops:
  0.7 28.2 %shard_map.64 = f32[64,128]{1,0:T(8,128)} custom-call(bf16[64,4096]{1,0:T(8,128)(2,1)} %q_hbm.1, bf16[512,4096]{1,0:T(8,128)(2,1)} %t_hbm.1, f32[1,4096]{1,0:T(1,128)} %bitcast.5, s32[1]{0:T(128)S(6)} %copy.8.counts_hbm, s32[1,256]{1,0:T(1,128)} %bitcast.6, s32[1,64]{1,0:T(1,128)} %bitcast.7), custom_call_target="tpu_custom_call" | custom-call | tf_op jit(solution)/shard_map/pallas_call | solution.py:354
  28.9 1.4 %copy.9 = f32[128,64]{0,1:T(8,128)} copy(f32[128,64]{0,1:T(8,128)} %bitcast.4) | data formatting | bytes 65536
